TPU v7x, 512 devices: a whole 4x8x8 slice. The times are simulated.
512 devices in a mesh: train: 64 (over z_lo, y, x), feat: 8 (over z_hi, core).
Axes of the slice: x: 4, y: 8, z: 8 (z_hi: 4, z_lo: 2; z = z_hi * 2 + z_lo), core: 2. Of those that a mesh axis runs over, the one named last changes fastest.
Arguments:
- train_grads: bfloat16 [32768, 8192], P('train', 'feat'), may hold values from -0.0625 to 0.0625
- query_grads: bfloat16 [2048, 8192], P('train', 'feat'), may hold values from -6 to 6
- precond: bfloat16 [8192, 1024], P('feat'), may hold values from -0.5 to 4.5, as said below
Outputs:
- scores: float32 [32768, 2048], P('train', 'feat')
Inputs may be any that keep to these rules, and one draw needn't show every extreme that they name: Each block of precond is symmetric.
All inputs are finite; a program needn't handle non-finite values.
Results may differ from a plain program's by a relative error of at most 0.0029.
Values may be sent and summed in bfloat16 or wider, within the bound.
A program may use at most 64 MiB of HBM per device.

v0:
```python
import jax
import jax.numpy as jnp
from jax import lax
from jax.sharding import PartitionSpec as P


def body(train_grads, query_grads, precond):
    width = precond.shape[1]
    local_feats = query_grads.shape[1]
    blocks = local_feats // width
    panel_rows = query_grads.shape[0]
    queries = query_grads.reshape(panel_rows, blocks, width)
    inverse = precond.reshape(blocks, width, width)
    pre = jnp.einsum("qbi,bij->qbj", queries, inverse, preferred_element_type=jnp.float32)
    pre = pre.reshape(panel_rows, local_feats).astype(jnp.bfloat16)
    contract = (((1,), (1,)), ((), ()))
    terms = lax.dot_general(
        train_grads,
        lax.all_gather(pre, "train", axis=0, tiled=True),
        contract,
        preferred_element_type=jnp.float32,
    )
    return lax.psum_scatter(terms, "feat", scatter_dimension=1, tiled=True)


def solution(mesh):
    placed = (P("train", "feat"), P("train", "feat"), P("feat", None))
    return jax.shard_map(
        body, mesh=mesh, in_specs=placed, out_specs=P("train", "feat"), check_vma=False
    )
```

profile of v0, /device:TPU:1, one launch (start us, length us, event | category | flops | bytes accessed | tf_op | source)
XLA Modules:
  0.0 395.6 jit_solution(1369013134300668972)
XLA Ops:
  6.5 0.0 copy-start
  6.5 0.0 all-gather.3.cloned.1.call-start
  6.5 1.6 copy-done
  8.1 1.9 fusion.5
  10.1 0.0 all-gather.3.cloned.1.call-update
  10.1 0.0 reduce-scatter.2.cloned.1.call-start
  10.1 268.5 %all-gather.3.cloned.1.call-done = bf16[2048,1,1024]{2,0,1:T(8,128)(2,1)} async-done(((bf16[32,1,1024]{2,0,1:T(8,128)(2,1)}), bf16[2048,1,1024]{2,0,1:T(8,128)(2,1)}) %all-gather.3.cloned.1.call-update) | async-done | bytes 4194320 | tf_op jit(solution)/shard_map/all_gather | solution.py:19
  278.7 6.8 %fusion.2 = f32[512,2048]{0,1:T(8,128)} fusion(bf16[512,1024]{1,0:T(8,128)(2,1)} %param.3, bf16[2048,1,1024]{2,0,1:T(8,128)(2,1)} %all-gather.3.cloned.1.call-done), kind=kOutput, calls=%fused_computation.2 | convolution fusion | flops 2147483648 | bytes 9437184 | tf_op jit(solution)/shard_map/dot_general | solution.py:17
  285.5 0.0 reduce-scatter.2.cloned.1.call-update
  285.5 101.2 %reduce-scatter.2.cloned.1.call-done = f32[512,256]{0,1:T(8,128)} async-done(((f32[512,2048]{0,1:T(8,128)}), f32[512,256]{0,1:T(8,128)}) %reduce-scatter.2.cloned.1.call-update) | async-done | bytes 524304 | tf_op jit(solution)/shard_map/reduce_scatter | solution.py:23
  386.7 2.0 copy.4
Async XLA Ops:
  6.5 1.6 copy-start
  6.5 272.1 %all-gather.3.cloned.1.call-start = ((), (), s32[]{:S(2)}) async-start(), calls=%async_computation.2 | async-start | bytes 4259840 | tf_op jit(solution)/shard_map/all_gather | solution.py:19
  10.1 376.6 %reduce-scatter.2.cloned.1.call-start = ((), (), s32[]{:S(2)}) async-start(), calls=%async_computation.1 | async-start | bytes 4718592 | tf_op jit(solution)/shard_map/reduce_scatter | solution.py:23
Sparse Core Ops, SparseCore 0:
  10.2 268.4 all-gather.2
  285.6 101.0 reduce-scatter.1
where the time goes:
time: 396 us
  waiting for transfers between devices  370 us (93%)
  between operations  13.4 us (3%)
  matrix products  8.75 us (2%)
    all_gather x1, waiting for transfers between devices, body(): lax.all_gather(pre, 'train', axis=0, tiled=True)  269 us
    reduce_scatter x1, waiting for transfers between devices, body(): return lax.psum_scatter(terms, 'feat', scatter_dimension=1, tiled=True)  101 us
  transfers between devices with their start and end apart: 2, of which 2 were waited for; matrix products, arithmetic and copies ran while one was open for 0% of the time, Pallas kernels for 0%

commit v1 on v0

v1 whole, which is shorter than its diff:
```python
import jax
import jax.numpy as jnp
from jax import lax
from jax.experimental import pallas as pl
from jax.experimental.pallas import tpu as pltpu
from jax.sharding import PartitionSpec as P

MESH = pl.DeviceIdType.MESH
XS, YS = 4, 8
ROWS, QROWS, W = 512, 32, 1024
CHUNK = XS * QROWS
KX = 768
XCOLS, YCOLS = pl.ds(0, KX), pl.ds(KX, 2 * W - KX)
NT = (((1,), (1,)), ((), ()))
X1, XY, YY, YX, Y2 = 0, 3, 35, 43, 59
N_TAGS = 75


def kernel(t_hbm, q_hbm, p_hbm, o_ref, prec, qry, pre, a, b, stage, lstage, local, parts,
           send, recv, load, init_s, init_r, a_s, a_r, rs_s, rs_r, l_s, l_r):
    t, f = lax.axis_index("train"), lax.axis_index("feat")
    x, y, zl = lax.rem(t, 4), lax.rem(t // 4, 8), t // 32
    zh, c = f // 2, lax.rem(f, 2)

    def dev(dx=0, dy=0, zlo=zl, zhi=zh, core=c):
        return (zlo * 32 + lax.rem(y + dy + 8, 8) * 4 + lax.rem(x + dx + 4, 4), zhi * 2 + core)

    def rows(dx=0, first=0, n=QROWS):
        return pl.ds(pl.multiple_of(lax.rem(x + dx + 4, 4) * QROWS + first, 16), n)

    def yi(dy):
        return lax.rem(y + dy + 8, 8)

    def panel(dy, dx, cols, first=0, n=QROWS):
        return b.at[yi(dy), rows(dx, first, n), cols]

    def copy(ref, tag, to):
        return pltpu.make_async_remote_copy(
            src_ref=ref, dst_ref=ref, send_sem=send.at[tag], recv_sem=recv.at[tag],
            device_id=to, device_id_type=MESH)

    started = []

    def go(ref, tag, to):
        cp = copy(ref, tag, to)
        cp.start()
        started.append(cp)

    def got(ref, tag):
        copy(ref, tag, dev()).wait_recv()

    half = pl.ds(pl.multiple_of(c * W, W), W)
    load_q = pltpu.make_async_copy(q_hbm, qry, load.at[0])
    load_p = pltpu.make_async_copy(p_hbm, prec, load.at[1])
    load_a = pltpu.make_async_copy(t_hbm, a.at[c], load.at[2])
    load_q.start()
    load_p.start()
    load_a.start()

    barrier = pltpu.get_barrier_semaphore()
    partners = [(t, lax.rem(f + i, 8)) for i in range(1, 8)]
    partners += [dev(dx=1), dev(dx=-1), dev(dx=2), dev(dy=1), dev(dy=-1)]
    partners += [dev(zlo=1 - zl, core=0), dev(zlo=1 - zl, core=1)]
    for partner in partners:
        pl.semaphore_signal(barrier, inc=1, device_id=partner, device_id_type=MESH)

    load_q.wait()
    load_p.wait()
    pre[...] = jnp.dot(qry[...], prec[...], preferred_element_type=jnp.float32).astype(jnp.bfloat16)
    pl.semaphore_wait(barrier, len(partners))

    mine = b.at[yi(0), rows(), half]

    def init(to, slot):
        return pltpu.make_async_remote_copy(
            src_ref=pre, dst_ref=mine, send_sem=init_s.at[slot], recv_sem=init_r.at[c],
            device_id=to, device_id_type=MESH)

    def init_got(h):
        dst = b.at[yi(0), rows(), pl.ds(pl.multiple_of(h * W, W), W)]
        pltpu.make_async_remote_copy(
            src_ref=pre, dst_ref=dst, send_sem=init_s.at[0], recv_sem=init_r.at[h],
            device_id=dev(), device_id_type=MESH).wait_recv()

    init_far = init(dev(zlo=1 - zl, core=zl), 0)
    init_near = init(dev(core=1 - c), 1)
    init_own = pltpu.make_async_copy(pre, mine, load.at[3])
    init_far.start()

    @pl.when(c == zl)
    def _():
        init_own.start()

    @pl.when(c != zl)
    def _():
        init_near.start()

    load_a.wait()
    a_copy = pltpu.make_async_remote_copy(
        src_ref=a.at[c], dst_ref=a.at[c], send_sem=a_s, recv_sem=a_r,
        device_id=dev(core=1 - c), device_id_type=MESH)
    a_copy.start()

    @pl.when(c == zl)
    def _():
        init_got(1 - c)
        init_own.wait()

    @pl.when(c != zl)
    def _():
        init_got(0)
        init_got(1)

    def chunk(i, dy):
        ys = yi(dy)
        acc = lax.dot_general(a[0], b[ys, :, pl.ds(0, W)], NT, preferred_element_type=jnp.float32)
        acc += lax.dot_general(a[1], b[ys, :, pl.ds(W, W)], NT, preferred_element_type=jnp.float32)
        owner, core, j = 2 * c + ys // 4, lax.rem(ys // 2, 2), lax.rem(ys, 2)

        @pl.when(owner != zh)
        def _():
            stage[i] = acc.astype(jnp.bfloat16)
            reduce_copy(i, dy).start()

        @pl.when(jnp.logical_and(owner == zh, core == c))
        def _():
            local[j] = acc

        @pl.when(jnp.logical_and(owner == zh, core != c))
        def _():
            lstage[j] = acc
            local_copy(j).start()

    def reduce_copy(i, dy):
        ys = yi(dy)
        owner, core, j = 2 * c + ys // 4, lax.rem(ys // 2, 2), lax.rem(ys, 2)
        slot = lax.rem(zh - owner + 3, 4)
        return pltpu.make_async_remote_copy(
            src_ref=stage.at[i], dst_ref=parts.at[slot, j], send_sem=rs_s.at[i], recv_sem=rs_r.at[slot, j],
            device_id=dev(zhi=owner, core=core), device_id_type=MESH)

    def local_copy(j):
        return pltpu.make_async_remote_copy(
            src_ref=lstage.at[j], dst_ref=local.at[j], send_sem=l_s.at[j], recv_sem=l_r.at[j],
            device_id=dev(core=1 - c), device_id_type=MESH)

    def chunks(k):
        def body(i, carry):
            chunk(2 * k - 1 + i, k * (1 - 2 * i))
            return carry
        lax.fori_loop(0, 2, body, 0)

    pieces = (0, 1, -1, 2)

    def xy_tag(d, k, p):
        return XY + (0 if d > 0 else 16) + k * 4 + p

    def xy_pieces(d, k):
        return range(4) if k < 3 else ((0, 3) if d > 0 else (1, 2))

    def xy_go(d, k, p):
        go(panel(-d * k, pieces[p], XCOLS), xy_tag(d, k, p), dev(dy=d))

    def xy_got(d, k, p):
        got(panel(-d * (k + 1), pieces[p], XCOLS), xy_tag(d, k, p))

    def yy_rows(d, k):
        return (0, QROWS) if k < 3 else ((0, 16) if d > 0 else (16, 16))

    def yy_go(d, k):
        go(panel(-d * k, 0, YCOLS, *yy_rows(d, k)), YY + (0 if d > 0 else 4) + k, dev(dy=d))

    def yy_got(d, k):
        got(panel(-d * (k + 1), 0, YCOLS, *yy_rows(d, k)), YY + (0 if d > 0 else 4) + k)

    def num(dy):
        return 0 if dy == 0 else 2 * abs(dy) - (1 if dy > 0 else 0)

    def yx_go(dy):
        for d in (1, -1):
            go(panel(dy, 0, YCOLS), YX + 2 * num(dy) + (0 if d > 0 else 1), dev(dx=d))

    def y2_forward(dy):
        for d in (1, -1):
            got(panel(dy, -d, YCOLS), YX + 2 * num(dy) + (0 if d > 0 else 1))
            first = 0 if d > 0 else 16
            go(panel(dy, -d, YCOLS, first, 16), Y2 + 2 * num(dy) + (0 if d > 0 else 1), dev(dx=d))

    def y2_got(dy):
        for d in (1, -1):
            first = 0 if d > 0 else 16
            got(panel(dy, 2, YCOLS, first, 16), Y2 + 2 * num(dy) + (0 if d > 0 else 1))

    def xy_stage(k):
        for d in (1, -1):
            for p in xy_pieces(d, k - 1):
                xy_got(d, k - 1, p)
                if k < 4 and p in xy_pieces(d, k):
                    xy_go(d, k, p)

    def yy_stage(k):
        for d in (1, -1):
            yy_got(d, k - 1)
            if k < 4:
                yy_go(d, k)
                yx_go(-d * k)
        if k == 4:
            yx_go(4)

    for d in (1, -1):
        yy_go(d, 0)
    for p in (1, 2, 3):
        go(panel(0, 0, XCOLS), X1 + p - 1, dev(dx=-pieces[p]))
    for d in (1, -1):
        xy_go(d, 0, 0)
    yx_go(0)
    yy_stage(1)
    for p in (1, 2, 3):
        got(panel(0, pieces[p], XCOLS), X1 + p - 1)
        for d in (1, -1):
            xy_go(d, 0, p)
    y2_forward(0)
    yy_stage(2)
    xy_stage(1)
    y2_got(0)
    a_copy.wait_recv()
    chunk(0, 0)
    for dy in (1, -1):
        y2_forward(dy)
    yy_stage(3)
    for dy in (1, -1):
        y2_got(dy)
    chunks(1)
    xy_stage(2)
    for dy in (2, -2):
        y2_forward(dy)
    yy_stage(4)
    for dy in (2, -2):
        y2_got(dy)
    chunks(2)
    xy_stage(3)
    for dy in (3, -3):
        y2_forward(dy)
    for dy in (3, -3):
        y2_got(dy)
    chunks(3)
    xy_stage(4)
    y2_forward(4)
    y2_got(4)
    chunk(7, 4)

    for cp in started:
        cp.wait_send()
    a_copy.wait_send()
    init_far.wait_send()

    @pl.when(c != zl)
    def _():
        init_near.wait_send()

    for i, dy in enumerate((0, 1, -1, 2, -2, 3, -3, 4)):
        @pl.when(2 * c + yi(dy) // 4 != zh)
        def _():
            reduce_copy(i, dy).wait_send()

    @pl.when(zh // 2 == c)
    def _():
        for j in range(2):
            local_copy(j).wait_send()

    @pl.when(zh // 2 != c)
    def _():
        for j in range(2):
            local_copy(j).wait_recv()

    for j in range(2):
        total = local[j]
        for slot in range(3):
            pltpu.make_async_remote_copy(
                src_ref=stage.at[0], dst_ref=parts.at[slot, j], send_sem=rs_s.at[0], recv_sem=rs_r.at[slot, j],
                device_id=dev(), device_id_type=MESH).wait_recv()
            total += parts[slot, j].astype(jnp.float32)
        o_ref[:, j * CHUNK:(j + 1) * CHUNK] = total


def body(train_grads, query_grads, precond):
    bf16, f32 = jnp.bfloat16, jnp.float32
    dma = pltpu.SemaphoreType.DMA
    return pl.pallas_call(
        kernel,
        out_shape=jax.ShapeDtypeStruct((ROWS, 2 * CHUNK), f32),
        in_specs=[pl.BlockSpec(memory_space=pl.ANY)] * 3,
        out_specs=pl.BlockSpec(memory_space=pltpu.VMEM),
        scratch_shapes=[
            pltpu.VMEM((W, W), bf16),
            pltpu.VMEM((QROWS, W), bf16),
            pltpu.VMEM((QROWS, W), bf16),
            pltpu.VMEM((2, ROWS, W), bf16),
            pltpu.VMEM((YS, CHUNK, 2 * W), bf16),
            pltpu.VMEM((YS, ROWS, CHUNK), bf16),
            pltpu.VMEM((2, ROWS, CHUNK), f32),
            pltpu.VMEM((2, ROWS, CHUNK), f32),
            pltpu.VMEM((3, 2, ROWS, CHUNK), bf16),
            dma((N_TAGS,)), dma((N_TAGS,)), dma((4,)), dma((2,)), dma((2,)), dma, dma,
            dma((YS,)), dma((3, 2)), dma((2,)), dma((2,)),
        ],
        compiler_params=pltpu.CompilerParams(
            collective_id=0, has_side_effects=True, vmem_limit_bytes=48 * 1024 * 1024),
        cost_estimate=pl.CostEstimate(flops=2 * 2 * W * W * ROWS, bytes_accessed=4 << 20, transcendentals=0),
    )(train_grads, query_grads, precond)


def solution(mesh):
    placed = (P("train", "feat"), P("train", "feat"), P("feat", None))
    return jax.shard_map(
        body, mesh=mesh, in_specs=placed, out_specs=P("train", "feat"), check_vma=False
    )
```

time: 396 us -> 65.6 us (0.17)
  the two profiles are of different devices: /device:TPU:1 before, /device:TPU:40 now
where the time goes in v1:
time: 65.6 us; the launch traced here: 65.4 us
  Pallas kernels  60.9 us (93%)
  local copies, waits for them, and re-layouts  4.45 us (7%)
    pallas_call x1, Pallas kernels, body(): pl.pallas_call(kernel, out_shape=jax.ShapeDtypeStruct((ROWS, 2 * CHUNK),...  60.9 us
    unnamed x7, local copies, waits for them, and re-layouts  4.45 us

profile of v1, /device:TPU:40, one launch (start us, length us, event | category | flops | bytes accessed | tf_op | source)
XLA Modules:
  0.0 65.4 jit_solution(13929304138142515720)
XLA Ops:
  0.0 0.0 copy-start
  0.0 1.6 %copy-done = bf16[1024,1024]{1,0:T(8,128)(2,1)S(1)} copy-done((bf16[1024,1024]{1,0:T(8,128)(2,1)S(1)}, bf16[1024,1024]{1,0:T(8,128)(2,1)}, u32[]{:S(2)}) %copy-start) | copy-done | bytes 2097176
  1.6 0.0 copy-start.1
  1.6 1.2 %copy-done.1 = bf16[512,1024]{1,0:T(8,128)(2,1)S(1)} copy-done((bf16[512,1024]{1,0:T(8,128)(2,1)S(1)}, bf16[512,1024]{1,0:T(8,128)(2,1)}, u32[]{:S(2)}) %copy-start.1) | copy-done | bytes 1048600
  2.8 0.0 copy-start.2
  2.8 0.8 %copy-done.2 = bf16[32,1024]{1,0:T(8,128)(2,1)S(1)} copy-done((bf16[32,1024]{1,0:T(8,128)(2,1)S(1)}, bf16[32,1024]{1,0:T(8,128)(2,1)}, u32[]{:S(2)}) %copy-start.2) | copy-done | bytes 65560
  3.7 60.9 %shard_map.37 = f32[512,256]{1,0:T(8,128)S(1)} custom-call(bf16[512,1024]{1,0:T(8,128)(2,1)S(1)} %copy-done.1, bf16[32,1024]{1,0:T(8,128)(2,1)S(1)} %copy-done.2, bf16[1024,1024]{1,0:T(8,128)(2,1)S(1)} %copy-done), custom_call_target="tpu_custom_call" | custom-call | flops 2147483648 | bytes 4194304 | tf_op jit(solution)/shard_map/pallas_call | solution.py:289
  64.6 0.8 %copy.5 = f32[512,256]{1,0:T(8,128)} copy(f32[512,256]{1,0:T(8,128)S(1)} %shard_map.37) | data formatting | bytes 1048576
Async XLA Ops:
  0.0 1.6 %copy-start = (bf16[1024,1024]{1,0:T(8,128)(2,1)S(1)}, bf16[1024,1024]{1,0:T(8,128)(2,1)}, u32[]{:S(2)}) copy-start(bf16[1024,1024]{1,0:T(8,128)(2,1)} %p_hbm.1) | copy-start | bytes 6291460
  1.6 1.2 %copy-start.1 = (bf16[512,1024]{1,0:T(8,128)(2,1)S(1)}, bf16[512,1024]{1,0:T(8,128)(2,1)}, u32[]{:S(2)}) copy-start(bf16[512,1024]{1,0:T(8,128)(2,1)} %t_hbm.1) | copy-start | bytes 3145732
  2.8 0.8 %copy-start.2 = (bf16[32,1024]{1,0:T(8,128)(2,1)S(1)}, bf16[32,1024]{1,0:T(8,128)(2,1)}, u32[]{:S(2)}) copy-start(bf16[32,1024]{1,0:T(8,128)(2,1)} %q_hbm.1) | copy-start | bytes 196612

commit v2 on v1

v2 whole, which is shorter than its diff:
```python
import jax
import jax.numpy as jnp
from jax import lax
from jax.experimental import pallas as pl
from jax.experimental.pallas import tpu as pltpu
from jax.sharding import PartitionSpec as P

MESH = pl.DeviceIdType.MESH
XS, YS = 4, 8
ROWS, QROWS, W = 512, 32, 1024
CHUNK = XS * QROWS
KX = 896
XCOLS, YCOLS = pl.ds(0, KX), pl.ds(KX, 2 * W - KX)
NT = (((1,), (1,)), ((), ()))
HALF = ROWS // 2
DIRECT = (4,)
PIECES = (0, 1, -1, 2)
DISTANCES = (0, 1, -1, 2, -2, 3, -3, 4)
RATE, HOP, AHEAD, RELAY = 46500.0, 1.9, 2.0, 5.5


def pieces_of(d, k):
    return range(4) if k < 3 else ((0, 3) if d > 0 else (1, 2))


def messages():
    ky, out = 2 * W - KX, {}
    for d in (1, -1):
        xl, yl = ("x", d), ("y", d)
        for k in range(4):
            out["yy", d, k] = ([yl], QROWS if k < 3 else 16, ky, [("yy", d, k - 1)] if k else [], k)
            for p in pieces_of(d, k):
                needs = [("xy", d, k - 1, p)] if k else [("x1", p)] if p else []
                out["xy", d, k, p] = ([yl], QROWS, KX, needs, 2 + 2 * k + 0.1 * p)
        for dy in DISTANCES:
            needs = [] if dy == 0 else [("yy", 1, 3), ("yy", -1, 3)] if dy == 4 else [("yy", 1 if dy < 0 else -1, abs(dy) - 1)]
            late = 2 * abs(dy) + (0.5 if dy < 0 else 0)
            out["yx", dy, d] = ([xl], QROWS, ky, needs, 1 + late)
            out["y2", dy, d] = ([xl], 16, ky, [("yx", dy, d)], 2.2 + late)
    out["x1", 1] = ([("x", -1)], QROWS, KX, [], 0)
    out["x1", 2] = ([("x", 1)], QROWS, KX, [], 0)
    out["x1", 3] = ([("x", 1), ("x", -1)], QROWS, KX, [], 0)
    return out


def needs_of(dy):
    out = [(n, dy, d) for d in (1, -1) for n in ("yx", "y2")]
    if dy == 0:
        return out + [("x1", p) for p in (1, 2, 3)]
    if dy == 4:
        return out + [("xy", d, 3, p) for d in (1, -1) for p in pieces_of(d, 3)] + [("yy", 1, 3), ("yy", -1, 3)]
    d, k = 1 if dy < 0 else -1, abs(dy) - 1
    return out + [("xy", d, k, p) for p in range(4)] + [("yy", d, k)]


def plan():
    todo, here, free, steps = messages(), {}, {}, []
    while todo:
        best = None
        for name, (links, n, cols, needs, late) in todo.items():
            if all(q in here for q in needs):
                ready = max([here[q] for q in needs], default=0.0)
                start = max([ready] + [free.get(link, 0.0) for link in links])
                if best is None or (start, late) < best[:2]:
                    best = (start, late, name, ready)
        start, _, name, ready = best
        links, n, cols, needs, _ = todo.pop(name)
        end = start + n * cols * 2 / RATE
        free.update({link: end for link in links})
        here[name] = end + HOP + 0.5 * (len(links) - 1)
        steps.append((max(ready, start - AHEAD), len(steps), "go", name, needs))
    for dy in DISTANCES:
        at = max(here[q] for q in needs_of(dy))
        steps.append((at, len(steps), "chunk", dy, needs_of(dy)))
        if dy not in DIRECT:
            steps.append((at + RELAY, len(steps), "relay", dy, []))
    return [step[2:] for step in sorted(steps)]


def kernel(t_hbm, q_hbm, p_hbm, o_ref, prec, qry, pre, a, b, stage, hold, relay, lstage, local, parts,
           send, recv, load, init_s, init_r, a_s, a_r, rs_s, rs_r, mid_s, mid_r, l_s, l_r):
    t, f = lax.axis_index("train"), lax.axis_index("feat")
    x, y, zl = lax.rem(t, 4), lax.rem(t // 4, 8), t // 32
    zh, c = f // 2, lax.rem(f, 2)

    def dev(dx=0, dy=0, zlo=zl, zhi=zh, core=c):
        return (zlo * 32 + lax.rem(y + dy + 8, 8) * 4 + lax.rem(x + dx + 4, 4), zhi * 2 + core)

    def rows(dx=0, first=0, n=QROWS):
        return pl.ds(pl.multiple_of(lax.rem(x + dx + 4, 4) * QROWS + first, 16), n)

    def yi(dy):
        return lax.rem(y + dy + 8, 8)

    def panel(dy, dx, cols, first=0, n=QROWS):
        return b.at[yi(dy), rows(dx, first, n), cols]

    def copy(ref, tag, to):
        return pltpu.make_async_remote_copy(
            src_ref=ref, dst_ref=ref, send_sem=send.at[tag], recv_sem=recv.at[tag],
            device_id=to, device_id_type=MESH)

    started = []

    def go(ref, tag, to):
        cp = copy(ref, tag, to)
        cp.start()
        started.append(cp)

    def got(ref, tag):
        copy(ref, tag, dev()).wait_recv()

    half = pl.ds(pl.multiple_of(c * W, W), W)
    load_q = pltpu.make_async_copy(q_hbm, qry, load.at[0])
    load_p = pltpu.make_async_copy(p_hbm, prec, load.at[1])
    load_a = pltpu.make_async_copy(t_hbm, a.at[c], load.at[2])
    load_q.start()
    load_p.start()
    load_a.start()

    barrier = pltpu.get_barrier_semaphore()
    partners = [(t, lax.rem(f + i, 8)) for i in range(1, 8)]
    partners += [dev(dx=1), dev(dx=-1), dev(dx=2), dev(dy=1), dev(dy=-1)]
    partners += [dev(zlo=1 - zl, core=0), dev(zlo=1 - zl, core=1)]
    for partner in partners:
        pl.semaphore_signal(barrier, inc=1, device_id=partner, device_id_type=MESH)

    load_q.wait()
    load_p.wait()
    pre[...] = jnp.dot(qry[...], prec[...], preferred_element_type=jnp.float32).astype(jnp.bfloat16)
    pl.semaphore_wait(barrier, len(partners))

    mine = b.at[yi(0), rows(), half]

    def init(to, slot):
        return pltpu.make_async_remote_copy(
            src_ref=pre, dst_ref=mine, send_sem=init_s.at[slot], recv_sem=init_r.at[c],
            device_id=to, device_id_type=MESH)

    def init_got(h):
        dst = b.at[yi(0), rows(), pl.ds(pl.multiple_of(h * W, W), W)]
        pltpu.make_async_remote_copy(
            src_ref=pre, dst_ref=dst, send_sem=init_s.at[0], recv_sem=init_r.at[h],
            device_id=dev(), device_id_type=MESH).wait_recv()

    init_far = init(dev(zlo=1 - zl, core=zl), 0)
    init_near = init(dev(core=1 - c), 1)
    init_own = pltpu.make_async_copy(pre, mine, load.at[3])
    init_far.start()

    @pl.when(c == zl)
    def _():
        init_own.start()

    @pl.when(c != zl)
    def _():
        init_near.start()

    load_a.wait()
    a_copy = pltpu.make_async_remote_copy(
        src_ref=a.at[c], dst_ref=a.at[c], send_sem=a_s, recv_sem=a_r,
        device_id=dev(core=1 - c), device_id_type=MESH)
    a_copy.start()

    @pl.when(c == zl)
    def _():
        init_got(1 - c)
        init_own.wait()

    @pl.when(c != zl)
    def _():
        init_got(0)
        init_got(1)

    def place(dy):
        ys = yi(dy)
        owner = 2 * c + ys // 4
        return owner, lax.rem(ys // 2, 2), lax.rem(ys, 2), lax.rem(zh - owner + 4, 4)

    def owner_copy(i, dy, slot, h, kind):
        owner, core, j, _ = place(dy)
        part = pl.ds(0, ROWS) if h is None else pl.ds(pl.multiple_of(h * HALF, HALF), HALF)
        return pltpu.make_async_remote_copy(
            src_ref=stage.at[i, part], dst_ref=parts.at[slot, j, part], send_sem=rs_s.at[kind, i],
            recv_sem=rs_r.at[kind, slot, j], device_id=dev(zhi=owner, core=core), device_id_type=MESH)

    def relay_copy(i, h):
        return pltpu.make_async_remote_copy(
            src_ref=stage.at[i, pl.ds(h * HALF, HALF)], dst_ref=relay.at[i], send_sem=mid_s.at[h, i], recv_sem=mid_r.at[i],
            device_id=dev(zhi=lax.rem(zh + (3, 1)[h], 4)), device_id_type=MESH)

    def local_copy(j):
        return pltpu.make_async_remote_copy(
            src_ref=lstage.at[j], dst_ref=local.at[j], send_sem=l_s.at[j], recv_sem=l_r.at[j],
            device_id=dev(core=1 - c), device_id_type=MESH)

    def chunk(i, dy):
        ys = yi(dy)
        acc = lax.dot_general(a[0], b[ys, :, pl.ds(0, W)], NT, preferred_element_type=jnp.float32)
        acc += lax.dot_general(a[1], b[ys, :, pl.ds(W, W)], NT, preferred_element_type=jnp.float32)
        owner, core, j, away = place(dy)

        if dy in DIRECT:
            @pl.when(away != 0)
            def _():
                stage[i] = acc.astype(jnp.bfloat16)
                owner_copy(i, dy, away - 1, None, 2).start()
        else:
            @pl.when(away == 2)
            def _():
                stage[i] = acc.astype(jnp.bfloat16)
                relay_copy(i, 0).start()
                relay_copy(i, 1).start()

            for h, at in ((0, 1), (1, 3)):
                @pl.when(away == at)
                def _():
                    now = pl.ds((1 - h) * HALF, HALF)
                    stage[i, now] = acc[(1 - h) * HALF:(2 - h) * HALF].astype(jnp.bfloat16)
                    owner_copy(i, dy, h, 1 - h, 0).start()
                    hold[i] = acc[h * HALF:(h + 1) * HALF]

        @pl.when(jnp.logical_and(away == 0, core == c))
        def _():
            local[j] = acc

        @pl.when(jnp.logical_and(away == 0, core != c))
        def _():
            lstage[j] = acc
            local_copy(j).start()

    def relayed(i, dy):
        _, _, _, away = place(dy)

        @pl.when(lax.rem(away, 2) == 1)
        def _():
            h = away // 2
            relay_copy(i, 0).wait_recv()
            later = pl.ds(pl.multiple_of(h * HALF, HALF), HALF)
            stage[i, later] = (hold[i] + relay[i].astype(jnp.float32)).astype(jnp.bfloat16)
            owner_copy(i, dy, h, h, 1).start()

    tags = {name: n for n, name in enumerate(messages())}

    def message(name):
        kind = name[0]
        if kind == "x1":
            p = PIECES[name[1]]
            return (0, 0, XCOLS), (0, p, XCOLS), dev(dx=-p)
        if kind == "xy":
            _, d, k, p = name
            return (-d * k, PIECES[p], XCOLS), (-d * (k + 1), PIECES[p], XCOLS), dev(dy=d)
        if kind == "yy":
            _, d, k = name
            part = (0, QROWS) if k < 3 else (0, 16) if d > 0 else (16, 16)
            return (-d * k, 0, YCOLS, *part), (-d * (k + 1), 0, YCOLS, *part), dev(dy=d)
        _, dy, d = name
        part = (0, QROWS) if kind == "yx" else (0, 16) if d > 0 else (16, 16)
        hops = 0 if kind == "yx" else 1
        return (dy, -d * hops, YCOLS, *part), (dy, -d * (hops + 1), YCOLS, *part), dev(dx=d)

    seen = set()
    for kind, what, needs in plan():
        for name in needs:
            if name not in seen:
                seen.add(name)
                got(panel(*message(name)[1]), tags[name])
        if kind == "go":
            block, _, to = message(what)
            go(panel(*block), tags[what], to)
        elif kind == "chunk":
            if what == 0:
                a_copy.wait_recv()
            chunk(DISTANCES.index(what), what)
        else:
            relayed(DISTANCES.index(what), what)

    for cp in started:
        cp.wait_send()
    a_copy.wait_send()
    init_far.wait_send()

    @pl.when(c != zl)
    def _():
        init_near.wait_send()

    for i, dy in enumerate(DISTANCES):
        _, _, _, away = place(dy)
        if dy in DIRECT:
            @pl.when(away != 0)
            def _():
                owner_copy(i, dy, 0, None, 2).wait_send()
        else:
            @pl.when(away == 2)
            def _():
                relay_copy(i, 0).wait_send()
                relay_copy(i, 1).wait_send()

            @pl.when(lax.rem(away, 2) == 1)
            def _():
                owner_copy(i, dy, 0, 0, 0).wait_send()
                owner_copy(i, dy, 0, 0, 1).wait_send()

    @pl.when(zh // 2 == c)
    def _():
        for j in range(2):
            local_copy(j).wait_send()

    @pl.when(zh // 2 != c)
    def _():
        for j in range(2):
            local_copy(j).wait_recv()

    def part_got(slot, j, h, kind):
        part = pl.ds(0, ROWS) if h is None else pl.ds(h * HALF, HALF)
        pltpu.make_async_remote_copy(
            src_ref=stage.at[0, part], dst_ref=parts.at[slot, j, part], send_sem=rs_s.at[0, 0],
            recv_sem=rs_r.at[kind, slot, j], device_id=dev(), device_id_type=MESH).wait_recv()

    for j in range(2):
        away = lax.rem(4 * lax.rem(zh, 2) + 2 * c + j - y + 8, 8)
        straight = away == DIRECT[0] % 8
        for d in DIRECT[1:]:
            straight = jnp.logical_or(straight, away == d % 8)
        cols = slice(j * CHUNK, (j + 1) * CHUNK)

        @pl.when(straight)
        def _():
            for slot in range(3):
                part_got(slot, j, None, 2)
            o_ref[:, cols] = local[j] + sum(parts[slot, j].astype(jnp.float32) for slot in range(3))

        @pl.when(jnp.logical_not(straight))
        def _():
            for h in range(2):
                part_got(h, j, 1 - h, 0)
                part_got(h, j, h, 1)
            o_ref[:, cols] = local[j] + parts[0, j].astype(jnp.float32) + parts[1, j].astype(jnp.float32)


def body(train_grads, query_grads, precond):
    bf16, f32 = jnp.bfloat16, jnp.float32
    dma = pltpu.SemaphoreType.DMA
    n_tags = len(messages())
    return pl.pallas_call(
        kernel,
        out_shape=jax.ShapeDtypeStruct((ROWS, 2 * CHUNK), f32),
        in_specs=[pl.BlockSpec(memory_space=pltpu.HBM)] * 3,
        out_specs=pl.BlockSpec(memory_space=pltpu.VMEM),
        scratch_shapes=[
            pltpu.VMEM((W, W), bf16),
            pltpu.VMEM((QROWS, W), bf16),
            pltpu.VMEM((QROWS, W), bf16),
            pltpu.VMEM((2, ROWS, W), bf16),
            pltpu.VMEM((YS, CHUNK, 2 * W), bf16),
            pltpu.VMEM((YS, ROWS, CHUNK), bf16),
            pltpu.VMEM((YS, HALF, CHUNK), f32),
            pltpu.VMEM((YS, HALF, CHUNK), bf16),
            pltpu.VMEM((2, ROWS, CHUNK), f32),
            pltpu.VMEM((2, ROWS, CHUNK), f32),
            pltpu.VMEM((3, 2, ROWS, CHUNK), bf16),
            dma((n_tags,)), dma((n_tags,)), dma((4,)), dma((2,)), dma((2,)), dma, dma,
            dma((3, YS)), dma((3, 3, 2)), dma((2, YS)), dma((YS,)), dma((2,)), dma((2,)),
        ],
        compiler_params=pltpu.CompilerParams(
            collective_id=0, has_side_effects=True, vmem_limit_bytes=60 * 1024 * 1024),
        cost_estimate=pl.CostEstimate(flops=2 * 2 * W * W * ROWS, bytes_accessed=4 << 20, transcendentals=0),
    )(train_grads, query_grads, precond)


def solution(mesh):
    placed = (P("train", "feat"), P("train", "feat"), P("feat", None))
    return jax.shard_map(
        body, mesh=mesh, in_specs=placed, out_specs=P("train", "feat"), check_vma=False
    )
```

time: 65.6 us -> 58 us (0.88)
  the two profiles are of different devices: /device:TPU:40 before, /device:TPU:88 now
where the time goes in v2:
time: 58 us; the launch traced here: 57.8 us
  Pallas kernels  56 us (97%)
  local copies, waits for them, and re-layouts  1.87 us (3%)
    pallas_call x1, Pallas kernels, body(): pl.pallas_call(kernel, out_shape=jax.ShapeDtypeStruct((ROWS, 2 * CHUNK),...  56 us
    unnamed x1, local copies, waits for them, and re-layouts  1.87 us

profile of v2, /device:TPU:88, one launch (start us, length us, event | category | flops | bytes accessed | tf_op | source)
XLA Modules:
  0.0 57.8 jit_solution(12595546998247334925)
XLA Ops:
  0.0 56.0 %shard_map.37 = f32[512,256]{1,0:T(8,128)} custom-call(bf16[512,1024]{1,0:T(8,128)(2,1)} %t_hbm.1, bf16[32,1024]{1,0:T(8,128)(2,1)} %q_hbm.1, bf16[1024,1024]{1,0:T(8,128)(2,1)} %p_hbm.1), custom_call_target="tpu_custom_call" | custom-call | flops 2147483648 | bytes 4194304 | tf_op jit(solution)/shard_map/pallas_call | solution.py:345
  56.0 1.9 %copy.5 = f32[512,256]{1,0:T(8,128)} copy(f32[512,256]{1,0:T(8,128)} %shard_map.37) | data formatting | bytes 1048576

commit v3 on v2

--- a/solution.py
+++ b/solution.py
@@ -1,3 +1,5 @@
+import functools
+
 import jax
 import jax.numpy as jnp
 from jax import lax
@@ -13,14 +15,14 @@
 XCOLS, YCOLS = pl.ds(0, KX), pl.ds(KX, 2 * W - KX)
 NT = (((1,), (1,)), ((), ()))
 HALF = ROWS // 2
-DIRECT = (4,)
+DIRECT = ()
 PIECES = (0, 1, -1, 2)
 DISTANCES = (0, 1, -1, 2, -2, 3, -3, 4)
 RATE, HOP, AHEAD, RELAY = 46500.0, 1.9, 2.0, 5.5
 
 
-def pieces_of(d, k):
-    return range(4) if k < 3 else ((0, 3) if d > 0 else (1, 2))
+def pieces_of(k):
+    return range(4) if k < 3 else range(2)
 
 
 def messages():
@@ -29,8 +31,8 @@
         xl, yl = ("x", d), ("y", d)
         for k in range(4):
             out["yy", d, k] = ([yl], QROWS if k < 3 else 16, ky, [("yy", d, k - 1)] if k else [], k)
-            for p in pieces_of(d, k):
-                needs = [("xy", d, k - 1, p)] if k else [("x1", p)] if p else []
+            for p in pieces_of(k):
+                needs = [("xy", d, 2, q) for q in range(4)] if k == 3 else [("xy", d, k - 1, p)] if k else [("x1", p)] if p else []
                 out["xy", d, k, p] = ([yl], QROWS, KX, needs, 2 + 2 * k + 0.1 * p)
         for dy in DISTANCES:
             needs = [] if dy == 0 else [("yy", 1, 3), ("yy", -1, 3)] if dy == 4 else [("yy", 1 if dy < 0 else -1, abs(dy) - 1)]
@@ -48,7 +50,7 @@
     if dy == 0:
         return out + [("x1", p) for p in (1, 2, 3)]
     if dy == 4:
-        return out + [("xy", d, 3, p) for d in (1, -1) for p in pieces_of(d, 3)] + [("yy", 1, 3), ("yy", -1, 3)]
+        return out + [("xy", d, 3, p) for d in (1, -1) for p in pieces_of(3)] + [("yy", 1, 3), ("yy", -1, 3)]
     d, k = 1 if dy < 0 else -1, abs(dy) - 1
     return out + [("xy", d, k, p) for p in range(4)] + [("yy", d, k)]
 
@@ -82,6 +84,10 @@
     t, f = lax.axis_index("train"), lax.axis_index("feat")
     x, y, zl = lax.rem(t, 4), lax.rem(t // 4, 8), t // 32
     zh, c = f // 2, lax.rem(f, 2)
+    mirror = 2 * (lax.rem(y, 4) // 2) - 1
+
+    def minus(d):
+        return (1 - mirror * d) // 2
 
     def dev(dx=0, dy=0, zlo=zl, zhi=zh, core=c):
         return (zlo * 32 + lax.rem(y + dy + 8, 8) * 4 + lax.rem(x + dx + 4, 4), zhi * 2 + core)
@@ -90,7 +96,7 @@
         return pl.ds(pl.multiple_of(lax.rem(x + dx + 4, 4) * QROWS + first, 16), n)
 
     def yi(dy):
-        return lax.rem(y + dy + 8, 8)
+        return lax.rem(y + mirror * dy + 8, 8)
 
     def panel(dy, dx, cols, first=0, n=QROWS):
         return b.at[yi(dy), rows(dx, first, n), cols]
@@ -240,7 +246,14 @@
             stage[i, later] = (hold[i] + relay[i].astype(jnp.float32)).astype(jnp.bfloat16)
             owner_copy(i, dy, h, h, 1).start()
 
-    tags = {name: n for n, name in enumerate(messages())}
+    names = list(messages())
+    per_way = [name for name in names if name[0] in ("yy", "xy") and name[1] > 0]
+    rest = [name for name in names if name[0] not in ("yy", "xy")]
+
+    def tag(name):
+        if name[0] in ("yy", "xy"):
+            return per_way.index((name[0], 1, *name[2:])) + len(per_way) * minus(name[1])
+        return 2 * len(per_way) + rest.index(name)
 
     def message(name):
         kind = name[0]
@@ -249,11 +262,12 @@
             return (0, 0, XCOLS), (0, p, XCOLS), dev(dx=-p)
         if kind == "xy":
             _, d, k, p = name
-            return (-d * k, PIECES[p], XCOLS), (-d * (k + 1), PIECES[p], XCOLS), dev(dy=d)
+            place_x = PIECES[p] if k < 3 else 2 * p + minus(d)
+            return (-d * k, place_x, XCOLS), (-d * (k + 1), place_x, XCOLS), dev(dy=mirror * d)
         if kind == "yy":
             _, d, k = name
-            part = (0, QROWS) if k < 3 else (0, 16) if d > 0 else (16, 16)
-            return (-d * k, 0, YCOLS, *part), (-d * (k + 1), 0, YCOLS, *part), dev(dy=d)
+            part = (0, QROWS) if k < 3 else (16 * minus(d), 16)
+            return (-d * k, 0, YCOLS, *part), (-d * (k + 1), 0, YCOLS, *part), dev(dy=mirror * d)
         _, dy, d = name
         part = (0, QROWS) if kind == "yx" else (0, 16) if d > 0 else (16, 16)
         hops = 0 if kind == "yx" else 1
@@ -264,10 +278,10 @@
         for name in needs:
             if name not in seen:
                 seen.add(name)
-                got(panel(*message(name)[1]), tags[name])
+                got(panel(*message(name)[1]), tag(name))
         if kind == "go":
             block, _, to = message(what)
-            go(panel(*block), tags[what], to)
+            go(panel(*block), tag(what), to)
         elif kind == "chunk":
             if what == 0:
                 a_copy.wait_recv()
@@ -318,10 +332,8 @@
             recv_sem=rs_r.at[kind, slot, j], device_id=dev(), device_id_type=MESH).wait_recv()
 
     for j in range(2):
-        away = lax.rem(4 * lax.rem(zh, 2) + 2 * c + j - y + 8, 8)
-        straight = away == DIRECT[0] % 8
-        for d in DIRECT[1:]:
-            straight = jnp.logical_or(straight, away == d % 8)
+        dy = lax.rem(mirror * (4 * lax.rem(zh, 2) + 2 * c + j - y) + 16, 8)
+        straight = functools.reduce(jnp.logical_or, [dy == d % 8 for d in DIRECT], dy < 0)
         cols = slice(j * CHUNK, (j + 1) * CHUNK)
 
         @pl.when(straight)
@@ -344,7 +356,7 @@
     n_tags = len(messages())
     return pl.pallas_call(
         kernel,
-        out_shape=jax.ShapeDtypeStruct((ROWS, 2 * CHUNK), f32),
+        out_shape=pltpu.VMEM((ROWS, 2 * CHUNK), f32),
         in_specs=[pl.BlockSpec(memory_space=pltpu.HBM)] * 3,
         out_specs=pl.BlockSpec(memory_space=pltpu.VMEM),
         scratch_shapes=[

time: 58 us -> 54.3 us (0.936)
  the two profiles are of different devices: /device:TPU:88 before, /device:TPU:1 now
where the time goes in v3:
time: 54.3 us; the launch traced here: 54 us
  Pallas kernels  53.2 us (98%)
  local copies, waits for them, and re-layouts  0.8 us (1%)
    pallas_call x1, Pallas kernels, body(): pl.pallas_call(kernel, out_shape=pltpu.VMEM((ROWS, 2 * CHUNK), f32), in_s...  53.2 us

profile of v3, /device:TPU:1, one launch (start us, length us, event | category | flops | bytes accessed | tf_op | source)
XLA Modules:
  0.0 54.0 jit_solution(14935932251761932964)
XLA Ops:
  0.0 53.2 %shard_map.37 = f32[512,256]{1,0:T(8,128)S(1)} custom-call(bf16[512,1024]{1,0:T(8,128)(2,1)} %t_hbm.1, bf16[32,1024]{1,0:T(8,128)(2,1)} %q_hbm.1, bf16[1024,1024]{1,0:T(8,128)(2,1)} %p_hbm.1), custom_call_target="tpu_custom_call" | custom-call | flops 2147483648 | bytes 4194304 | tf_op jit(solution)/shard_map/pallas_call | solution.py:357
  53.2 0.8 %copy.5 = f32[512,256]{1,0:T(8,128)} copy(f32[512,256]{1,0:T(8,128)S(1)} %shard_map.37) | data formatting | bytes 1048576

commit v4 on v3

v4 whole, which is shorter than its diff:
```python
import jax
import jax.numpy as jnp
from jax import lax
from jax.experimental import pallas as pl
from jax.experimental.pallas import tpu as pltpu
from jax.sharding import PartitionSpec as P

MESH = pl.DeviceIdType.MESH
XS, YS = 4, 8
ROWS, QROWS, W = 512, 32, 1024
CHUNK = XS * QROWS
KX = 896
XCOLS, YCOLS = pl.ds(0, KX), pl.ds(KX, 2 * W - KX)
NT = (((1,), (1,)), ((), ()))
PIECES = (0, 1, -1, 2)
DISTANCES = (0, 1, -1, 2, -2, 3, -3, 4)
UNITS = tuple((dy, None) for dy in DISTANCES[:-1]) + ((4, 0), (4, 1))
STRAIGHT = ()
RATE, HOP, AHEAD, RELAY = 46500.0, 1.9, 2.0, 6.2


def pieces_of(k):
    return range(4) if k < 3 else range(2)


def messages():
    ky, out = 2 * W - KX, {}
    for d in (1, -1):
        xl, yl = ("x", d), ("y", d)
        for k in range(4):
            out["yy", d, k] = ([yl], QROWS if k < 3 else 16, ky, [("yy", d, k - 1)] if k else [], k)
            for p in pieces_of(k):
                needs = [("xy", d, 2, q + p) for q in range(3)] if k == 3 else [("xy", d, k - 1, p)] if k else [("x1", p)] if p else []
                out["xy", d, k, p] = ([yl], QROWS, KX, needs, 2 + 2 * k + 0.1 * p)
        for dy in DISTANCES:
            needs = [] if dy == 0 else [("yy", 1, 3), ("yy", -1, 3)] if dy == 4 else [("yy", 1 if dy < 0 else -1, abs(dy) - 1)]
            late = 2 * abs(dy) + (0.5 if dy < 0 else 0)
            out["yx", dy, d] = ([xl], QROWS, ky, needs, 1 + late)
            out["y2", dy, d] = ([xl], 16, ky, [("yx", dy, d)], 2.2 + late)
    out["x1", 1] = ([("x", -1)], QROWS, KX, [], 0)
    out["x1", 2] = ([("x", 1)], QROWS, KX, [], 0)
    out["x1", 3] = ([("x", 1), ("x", -1)], QROWS, KX, [], 0)
    return out


def needs_of(dy, half=1):
    out = [("yx", dy, d) for d in (1, -1)] + [("y2", dy, d) for d in (1, -1) if half]
    if dy == 0:
        return out + [("x1", p) for p in (1, 2, 3)]
    if dy == 4:
        return out + [(n, d, 3, *q) for d in (1, -1) for n, q in [("yy", ())] + [("xy", (p,)) for p in range(half + 1)]]
    d, k = 1 if dy < 0 else -1, abs(dy) - 1
    return out + [("xy", d, k, p) for p in range(4)] + [("yy", d, k)]


def plan():
    todo, here, free, steps = messages(), {}, {}, []
    while todo:
        best = None
        for name, (links, n, cols, needs, late) in todo.items():
            if all(q in here for q in needs):
                ready = max([here[q] for q in needs], default=0.0)
                start = max([ready] + [free.get(link, 0.0) for link in links])
                if best is None or (start, late) < best[:2]:
                    best = (start, late, name, ready)
        start, _, name, ready = best
        links, n, cols, needs, _ = todo.pop(name)
        end = start + n * cols * 2 / RATE
        free.update({link: end for link in links})
        here[name] = end + HOP + 0.5 * (len(links) - 1)
        steps.append((max(ready, start - AHEAD), len(steps), "go", name, needs))
    for unit in UNITS:
        dy, half = unit
        needs = needs_of(dy) if half is None else needs_of(dy, half)
        at = max(here[q] for q in needs)
        steps.append((at, len(steps), "chunk", unit, needs))
        if unit not in STRAIGHT:
            steps.append((at + RELAY, len(steps), "relay", unit, []))
    steps.append((at, len(steps), "sent", None, []))
    return [step[2:] for step in sorted(steps)]


def kernel(t_hbm, q_hbm, p_hbm, o_ref, prec, qry, pre, a, b, stage, hold, relay, lstage, local, parts, lstage2, local2, parts2,
           send, recv, load, init_s, init_r, a_s, a_r, rs_s, rs_r, rs2_r, mid_s, mid_r, l_s, l_r):
    t, f = lax.axis_index("train"), lax.axis_index("feat")
    x, y, zl = lax.rem(t, 4), lax.rem(t // 4, 8), t // 32
    zh, c = f // 2, lax.rem(f, 2)
    serves = lax.rem(c + zl, 2)
    mirror = 2 * (lax.rem(y, 4) // 2) - 1

    def minus(d):
        return (1 - mirror * d) // 2

    def dev(dx=0, dy=0, zlo=zl, zhi=zh, core=c):
        return (zlo * 32 + lax.rem(y + dy + 8, 8) * 4 + lax.rem(x + dx + 4, 4), zhi * 2 + core)

    def rows(dx=0, first=0, n=QROWS):
        return pl.ds(pl.multiple_of(lax.rem(x + dx + 4, 4) * QROWS + first, 16), n)

    def yi(dy):
        return lax.rem(y + mirror * dy + 8, 8)

    def panel(dy, dx, cols, first=0, n=QROWS):
        return b.at[yi(dy), rows(dx, first, n), cols]

    def copy(ref, tag, to):
        return pltpu.make_async_remote_copy(
            src_ref=ref, dst_ref=ref, send_sem=send.at[tag], recv_sem=recv.at[tag],
            device_id=to, device_id_type=MESH)

    started = []

    def go(ref, tag, to):
        cp = copy(ref, tag, to)
        cp.start()
        started.append(cp)

    def got(ref, tag):
        copy(ref, tag, dev()).wait_recv()

    half = pl.ds(pl.multiple_of(c * W, W), W)
    load_q = pltpu.make_async_copy(q_hbm, qry, load.at[0])
    load_p = pltpu.make_async_copy(p_hbm, prec, load.at[1])
    load_a = pltpu.make_async_copy(t_hbm, a.at[c], load.at[2])
    load_q.start()
    load_p.start()
    load_a.start()

    barrier = pltpu.get_barrier_semaphore()
    partners = [dev(zhi=lax.rem(zh + i, 4), core=k) for i in (1, 3) for k in range(2)] + [dev(core=1 - c)]
    partners += [dev(dx=1), dev(dx=-1), dev(dx=2), dev(dy=1), dev(dy=-1)]
    partners += [dev(zlo=1 - zl, core=0), dev(zlo=1 - zl, core=1)]
    for partner in partners:
        pl.semaphore_signal(barrier, inc=1, device_id=partner, device_id_type=MESH)

    load_q.wait()
    load_p.wait()
    pre[...] = jnp.dot(qry[...], prec[...], preferred_element_type=jnp.float32).astype(jnp.bfloat16)
    pl.semaphore_wait(barrier, len(partners))

    mine = b.at[yi(0), rows(), half]

    def init(to, slot):
        return pltpu.make_async_remote_copy(
            src_ref=pre, dst_ref=mine, send_sem=init_s.at[slot], recv_sem=init_r.at[c],
            device_id=to, device_id_type=MESH)

    def init_got(h):
        dst = b.at[yi(0), rows(), pl.ds(pl.multiple_of(h * W, W), W)]
        pltpu.make_async_remote_copy(
            src_ref=pre, dst_ref=dst, send_sem=init_s.at[0], recv_sem=init_r.at[h],
            device_id=dev(), device_id_type=MESH).wait_recv()

    init_far = init(dev(zlo=1 - zl, core=1), 0)
    init_near = init(dev(core=1 - c), 1)
    init_own = pltpu.make_async_copy(pre, mine, load.at[3])
    init_far.start()

    @pl.when(c == 0)
    def _():
        init_own.start()

    @pl.when(c != 0)
    def _():
        init_near.start()

    load_a.wait()
    a_copy = pltpu.make_async_remote_copy(
        src_ref=a.at[c], dst_ref=a.at[c], send_sem=a_s, recv_sem=a_r,
        device_id=dev(core=1 - c), device_id_type=MESH)
    a_copy.start()

    @pl.when(c == 0)
    def _():
        init_got(1)
        init_own.wait()

    @pl.when(c != 0)
    def _():
        init_got(0)
        init_got(1)

    def place(dy):
        ys = yi(dy)
        owner = 2 * serves + ys // 4
        return owner, lax.rem(ys // 2, 2), lax.rem(ys, 2), lax.rem(zh - owner + 4, 4)

    def height(unit):
        return ROWS if unit[1] is None else ROWS // 2

    def landing(unit, slot, j, part, kind):
        if unit[1] is None:
            return parts.at[slot, j, part], rs_r.at[kind, slot, j]
        return parts2.at[slot, unit[1], part], rs2_r.at[kind, slot, unit[1]]

    def part_of(unit, h):
        n = height(unit)
        return pl.ds(0, n) if h is None else pl.ds(pl.multiple_of(h * (n // 2), n // 2), n // 2)

    def owner_copy(unit, slot, h, kind):
        owner, core, j, _ = place(unit[0])
        i, part = UNITS.index(unit), part_of(unit, h)
        dst, sem = landing(unit, slot, j, part, kind)
        return pltpu.make_async_remote_copy(
            src_ref=stage.at[i, part], dst_ref=dst, send_sem=rs_s.at[kind, i], recv_sem=sem,
            device_id=dev(zhi=owner, core=core), device_id_type=MESH)

    def relay_copy(unit, h):
        i = UNITS.index(unit)
        return pltpu.make_async_remote_copy(
            src_ref=stage.at[i, part_of(unit, h)], dst_ref=relay.at[i, pl.ds(0, height(unit) // 2)],
            send_sem=mid_s.at[h, i], recv_sem=mid_r.at[i],
            device_id=dev(zhi=lax.rem(zh + (3, 1)[h], 4)), device_id_type=MESH)

    def local_copy(half, j):
        src, dst, k = (lstage.at[j], local.at[j], j) if half is None else (lstage2.at[half], local2.at[half], 2 + half)
        return pltpu.make_async_remote_copy(
            src_ref=src, dst_ref=dst, send_sem=l_s.at[k], recv_sem=l_r.at[k],
            device_id=dev(core=1 - c), device_id_type=MESH)

    def pair(half):
        low = x // 2 if half == 0 else 1 - x // 2
        return pl.ds(pl.multiple_of(low * CHUNK // 2, CHUNK // 2), CHUNK // 2)

    def chunk(unit):
        dy, half = unit
        i, n, ys = UNITS.index(unit), height(unit), yi(dy)
        these = slice(None) if half is None else pair(half)
        acc = lax.dot_general(a[0], b[ys, these, pl.ds(0, W)], NT, preferred_element_type=jnp.float32)
        acc += lax.dot_general(a[1], b[ys, these, pl.ds(W, W)], NT, preferred_element_type=jnp.float32)
        if half is not None:
            acc = jnp.concatenate([acc[:n], acc[n:]], axis=1)
        owner, core, j, away = place(dy)

        if unit in STRAIGHT:
            @pl.when(away != 0)
            def _():
                stage[i, :n] = acc.astype(jnp.bfloat16)
                owner_copy(unit, away - 1, None, 2).start()
        else:
            @pl.when(away == 2)
            def _():
                stage[i, :n] = acc.astype(jnp.bfloat16)
                relay_copy(unit, 0).start()
                relay_copy(unit, 1).start()

            for h, at in ((0, 1), (1, 3)):
                @pl.when(away == at)
                def _():
                    stage[i, part_of(unit, 1 - h)] = acc[(1 - h) * (n // 2):(2 - h) * (n // 2)].astype(jnp.bfloat16)
                    owner_copy(unit, 2 * h, 1 - h, 0).start()
                    hold[i, :n // 2] = acc[h * (n // 2):(h + 1) * (n // 2)]

        @pl.when(jnp.logical_and(away == 0, core == c))
        def _():
            if half is None:
                local[j] = acc
            else:
                local2[half] = acc

        @pl.when(jnp.logical_and(away == 0, core != c))
        def _():
            if half is None:
                lstage[j] = acc
            else:
                lstage2[half] = acc
            local_copy(half, j).start()

    def relayed(unit):
        i, n = UNITS.index(unit), height(unit)
        _, _, _, away = place(unit[0])

        @pl.when(lax.rem(away, 2) == 1)
        def _():
            h = away // 2
            relay_copy(unit, 0).wait_recv()
            stage[i, part_of(unit, h)] = (hold[i, :n // 2] + relay[i, :n // 2].astype(jnp.float32)).astype(jnp.bfloat16)
            owner_copy(unit, 2 * h, h, 1).start()

    names = list(messages())
    per_way = [name for name in names if name[0] in ("yy", "xy") and name[1] > 0]
    rest = [name for name in names if name[0] not in ("yy", "xy")]

    def tag(name):
        if name[0] in ("yy", "xy"):
            return per_way.index((name[0], 1, *name[2:])) + len(per_way) * minus(name[1])
        return 2 * len(per_way) + rest.index(name)

    def message(name):
        kind = name[0]
        if kind == "x1":
            p = PIECES[name[1]]
            return (0, 0, XCOLS), (0, p, XCOLS), dev(dx=-p)
        if kind == "xy":
            _, d, k, p = name
            place_x = PIECES[p] if k < 3 else (1 - minus(d)) * 2 * p + minus(d) * (1 - 2 * p) * (1 - 2 * lax.rem(x, 2))
            return (-d * k, place_x, XCOLS), (-d * (k + 1), place_x, XCOLS), dev(dy=mirror * d)
        if kind == "yy":
            _, d, k = name
            part = (0, QROWS) if k < 3 else (16 * minus(d), 16)
            return (-d * k, 0, YCOLS, *part), (-d * (k + 1), 0, YCOLS, *part), dev(dy=mirror * d)
        _, dy, d = name
        part = (0, QROWS) if kind == "yx" else (0, 16) if d > 0 else (16, 16)
        hops = 0 if kind == "yx" else 1
        return (dy, -d * hops, YCOLS, *part), (dy, -d * (hops + 1), YCOLS, *part), dev(dx=d)

    def sent():
        for cp in started:
            cp.wait_send()
        a_copy.wait_send()
        init_far.wait_send()

        @pl.when(c != 0)
        def _():
            init_near.wait_send()

    seen = set()
    for kind, what, needs in plan():
        for name in needs:
            if name not in seen:
                seen.add(name)
                got(panel(*message(name)[1]), tag(name))
        if kind == "go":
            block, _, to = message(what)
            go(panel(*block), tag(what), to)
        elif kind == "chunk":
            if what == UNITS[0]:
                a_copy.wait_recv()
            chunk(what)
        elif kind == "relay":
            relayed(what)
        else:
            sent()

    for unit in UNITS:
        _, _, j, away = place(unit[0])
        if unit in STRAIGHT:
            @pl.when(away != 0)
            def _():
                owner_copy(unit, 0, None, 2).wait_send()
        else:
            @pl.when(away == 2)
            def _():
                relay_copy(unit, 0).wait_send()
                relay_copy(unit, 1).wait_send()

            @pl.when(lax.rem(away, 2) == 1)
            def _():
                owner_copy(unit, 0, 0, 0).wait_send()
                owner_copy(unit, 0, 0, 1).wait_send()

        _, core, j, _ = place(unit[0])

        @pl.when(jnp.logical_and(away == 0, core != c))
        def _():
            local_copy(unit[1], j).wait_send()

    def part_got(unit, slot, j, h, kind):
        part = part_of(unit, h)
        dst, sem = landing(unit, slot, j, part, kind)
        pltpu.make_async_remote_copy(
            src_ref=stage.at[0, part], dst_ref=dst, send_sem=rs_s.at[0, 0], recv_sem=sem,
            device_id=dev(), device_id_type=MESH).wait_recv()

    def collect(unit, j):
        @pl.when(zh // 2 != serves)
        def _():
            local_copy(unit[1], j).wait_recv()

        if unit in STRAIGHT:
            for slot in range(3):
                part_got(unit, slot, j, None, 2)
        else:
            for h in range(2):
                part_got(unit, 2 * h, j, 1 - h, 0)
                part_got(unit, 2 * h, j, h, 1)
        own, come = (local[j], parts.at[:, j]) if unit[1] is None else (local2[unit[1]], parts2.at[:, unit[1]])
        return own + sum(come[slot].astype(jnp.float32) for slot in ((0, 1, 2) if unit in STRAIGHT else (0, 2)))

    for j in range(2):
        far = lax.rem(4 * lax.rem(zh, 2) + 2 * c + j - y + 8, 8) == 4
        cols = slice(j * CHUNK, (j + 1) * CHUNK)

        @pl.when(jnp.logical_not(far))
        def _():
            o_ref[:, cols] = collect(UNITS[0], j)

        @pl.when(far)
        def _():
            mine, other = collect((4, 0), j), collect((4, 1), j)
            first = x // 2 == 0
            left, right = jnp.where(first, mine, other), jnp.where(first, other, mine)
            half = CHUNK // 2
            o_ref[:ROWS // 2, cols] = jnp.concatenate([left[:, :half], right[:, :half]], axis=1)
            o_ref[ROWS // 2:, cols] = jnp.concatenate([left[:, half:], right[:, half:]], axis=1)


def body(train_grads, query_grads, precond):
    bf16, f32 = jnp.bfloat16, jnp.float32
    dma = pltpu.SemaphoreType.DMA
    n_tags = len(messages())
    return pl.pallas_call(
        kernel,
        out_shape=pltpu.VMEM((ROWS, 2 * CHUNK), f32),
        in_specs=[pl.BlockSpec(memory_space=pltpu.HBM)] * 3,
        out_specs=pl.BlockSpec(memory_space=pltpu.VMEM),
        scratch_shapes=[
            pltpu.VMEM((W, W), bf16),
            pltpu.VMEM((QROWS, W), bf16),
            pltpu.VMEM((QROWS, W), bf16),
            pltpu.VMEM((2, ROWS, W), bf16),
            pltpu.VMEM((YS, CHUNK, 2 * W), bf16),
            pltpu.VMEM((len(UNITS), ROWS, CHUNK), bf16),
            pltpu.VMEM((len(UNITS), ROWS // 2, CHUNK), f32),
            pltpu.VMEM((len(UNITS), ROWS // 2, CHUNK), bf16),
            pltpu.VMEM((2, ROWS, CHUNK), f32),
            pltpu.VMEM((2, ROWS, CHUNK), f32),
            pltpu.VMEM((3, 2, ROWS, CHUNK), bf16),
            pltpu.VMEM((2, ROWS // 2, CHUNK), f32),
            pltpu.VMEM((2, ROWS // 2, CHUNK), f32),
            pltpu.VMEM((3, 2, ROWS // 2, CHUNK), bf16),
            dma((n_tags,)), dma((n_tags,)), dma((4,)), dma((2,)), dma((2,)), dma, dma,
            dma((3, len(UNITS))), dma((2, 3, 2)), dma((3, 3, 2)), dma((2, len(UNITS))), dma((len(UNITS),)), dma((4,)), dma((4,)),
        ],
        compiler_params=pltpu.CompilerParams(
            collective_id=0, has_side_effects=True, vmem_limit_bytes=60 * 1024 * 1024),
        cost_estimate=pl.CostEstimate(flops=2 * 2 * W * W * ROWS, bytes_accessed=4 << 20, transcendentals=0),
    )(train_grads, query_grads, precond)


def solution(mesh):
    placed = (P("train", "feat"), P("train", "feat"), P("feat", None))
    return jax.shard_map(
        body, mesh=mesh, in_specs=placed, out_specs=P("train", "feat"), check_vma=False
    )
```

time: 54.3 us -> 52.8 us (0.972)
  Pallas kernels: 53.2 us -> 51.9 us
    pallas_call x1, Pallas kernels: 53.2 us -> 51.9 us  [body(): pl.pallas_call(kernel, out_shape=pltpu.VMEM((ROWS, 2 * CHUNK), f32), in_s...]
where the time goes in v4:
time: 52.8 us; the launch traced here: 52.7 us
  Pallas kernels  51.9 us (98%)
  local copies, waits for them, and re-layouts  0.8 us (2%)
    pallas_call x1, Pallas kernels, body(): pl.pallas_call(kernel, out_shape=pltpu.VMEM((ROWS, 2 * CHUNK), f32), in_s...  51.9 us

profile of v4, /device:TPU:1, one launch (start us, length us, event | category | flops | bytes accessed | tf_op | source)
XLA Modules:
  0.0 52.7 jit_solution(16721253420113658600)
XLA Ops:
  0.0 51.9 %shard_map.37 = f32[512,256]{1,0:T(8,128)S(1)} custom-call(bf16[512,1024]{1,0:T(8,128)(2,1)} %t_hbm.1, bf16[32,1024]{1,0:T(8,128)(2,1)} %q_hbm.1, bf16[1024,1024]{1,0:T(8,128)(2,1)} %p_hbm.1), custom_call_target="tpu_custom_call" | custom-call | flops 2147483648 | bytes 4194304 | tf_op jit(solution)/shard_map/pallas_call | solution.py:402
  51.9 0.8 %copy.5 = f32[512,256]{1,0:T(8,128)} copy(f32[512,256]{1,0:T(8,128)S(1)} %shard_map.37) | data formatting | bytes 1048576

commit v5 on v4

--- a/solution.py
+++ b/solution.py
@@ -75,7 +75,7 @@
         at = max(here[q] for q in needs)
         steps.append((at, len(steps), "chunk", unit, needs))
         if unit not in STRAIGHT:
-            steps.append((at + RELAY, len(steps), "relay", unit, []))
+            steps.append((at + (RELAY if abs(dy) < 3 else 4.0), len(steps), "relay", unit, []))
     steps.append((at, len(steps), "sent", None, []))
     return [step[2:] for step in sorted(steps)]
 
@@ -168,7 +168,6 @@
     a_copy = pltpu.make_async_remote_copy(
         src_ref=a.at[c], dst_ref=a.at[c], send_sem=a_s, recv_sem=a_r,
         device_id=dev(core=1 - c), device_id_type=MESH)
-    a_copy.start()
 
     @pl.when(c == 0)
     def _():
@@ -315,7 +314,9 @@
             init_near.wait_send()
 
     seen = set()
-    for kind, what, needs in plan():
+    for step, (kind, what, needs) in enumerate(plan()):
+        if step == 20:
+            a_copy.start()
         for name in needs:
             if name not in seen:
                 seen.add(name)

time: 52.8 us -> 52.8 us (level)
  no operation moved by 1% of the time
where the time goes in v5:
time: 52.8 us; the launch traced here: 52.7 us
  Pallas kernels  51.9 us (98%)
  local copies, waits for them, and re-layouts  0.8 us (2%)
    pallas_call x1, Pallas kernels, body(): pl.pallas_call(kernel, out_shape=pltpu.VMEM((ROWS, 2 * CHUNK), f32), in_s...  51.9 us

profile of v5, /device:TPU:1, one launch (start us, length us, event | category | flops | bytes accessed | tf_op | source)
XLA Modules:
  0.0 52.7 jit_solution(8220791819085343718)
XLA Ops:
  0.0 51.9 %shard_map.37 = f32[512,256]{1,0:T(8,128)S(1)} custom-call(bf16[512,1024]{1,0:T(8,128)(2,1)} %t_hbm.1, bf16[32,1024]{1,0:T(8,128)(2,1)} %q_hbm.1, bf16[1024,1024]{1,0:T(8,128)(2,1)} %p_hbm.1), custom_call_target="tpu_custom_call" | custom-call | flops 2147483648 | bytes 4194304 | tf_op jit(solution)/shard_map/pallas_call | solution.py:403
  51.9 0.8 %copy.5 = f32[512,256]{1,0:T(8,128)} copy(f32[512,256]{1,0:T(8,128)S(1)} %shard_map.37) | data formatting | bytes 1048576
